TPU v7x, 32 devices: a whole 2x2x4 slice. The times are simulated.
32 devices in a mesh: section: 2 (over x), dp: 16 (over z, y, core).
Axes of the slice: x: 2, y: 2, z: 4, core: 2. Of those that a mesh axis runs over, the one named last changes fastest.
Arguments:
- acts: float32 [2, 2, 16, 256, 768], P('section', None, 'dp'), may hold values from -6 to 6
- w_attn: bfloat16 [2, 768, 3072], P('section', 'dp'), may hold values from -4 to 4, as said below
- w_extra: bfloat16 [2, 768, 1536], P('section', 'dp'), may hold values from -4 to 4, as said below
- w_in: bfloat16 [2, 768, 4096], P('section', 'dp'), may hold values from -0.21875 to 0.21875
- w_out: bfloat16 [2, 2048, 768], P('section', 'dp'), may hold values from -0.125 to 0.125
- gains: bfloat16 [2, 3, 768], P('section', None, 'dp'), may hold values from 0.099609375 to 1.8984375
- segments: int32 [2, 16, 256], P(None, 'dp'), may hold values from 0 to 7, never falling along the last dimension, each value on 1 to 64 neighbouring positions
- cotangent: float32 [2, 2, 16, 256, 768], P('section', None, 'dp'), may hold values from -6 to 6
Outputs:
- outputs: float32 [2, 2, 16, 256, 768], P('section', None, 'dp')
- input_grad: float32 [2, 2, 16, 256, 768], P('section', None, 'dp')
- grad_attn: float32 [2, 768, 3072], P('section', 'dp')
- grad_extra: float32 [2, 768, 1536], P('section', 'dp')
- grad_in: float32 [2, 768, 4096], P('section', 'dp')
- grad_out: float32 [2, 2048, 768], P('section', 'dp')
- grad_gains: float32 [2, 3, 768], P('section', None, 'dp')
Inputs may be any that keep to these rules, and one draw needn't show every extreme that they name: `segments`: along each decoder row the answer numbers never fall; each answer spans 1 to 64 tokens. `w_attn`: independent entries. `w_extra`: independent entries.
All inputs are finite; a program needn't handle non-finite values.
Results may differ from a plain program's by a relative error of at most 0.015.
Values may be sent and summed in bfloat16 or wider, within the bound.
A program may use at most 448 MiB of HBM per device.

v0:
```python
import jax
import jax.numpy as jnp
from jax import lax
from jax.sharding import PartitionSpec as P

D = 768
HEADS = 12
HDIM = 64
FF = 2048
SEQ = 256
MICRO = 2


def from_behind(block, axis, distance):
    devices = range(lax.axis_size(axis))
    route = [(i - distance, i) for i in devices if i - distance in devices]
    return lax.ppermute(block, axis, route)


def rms_norm(activations, gain_row):
    return (
        activations
        * lax.rsqrt(jnp.mean(activations * activations, axis=-1, keepdims=True) + 1e-06)
        * gain_row
    )


def project(left_side, right_side):
    return jnp.dot(left_side, right_side, preferred_element_type=jnp.float32)


def weight_grad(left_side, right_side):
    return jnp.einsum("sd,se->de", left_side, right_side, preferred_element_type=jnp.float32)


def input_back(gradient, weight):
    return jnp.einsum("se,de->sd", gradient, weight, preferred_element_type=jnp.float32)


def norm_back(activations, gain_row, gradient):
    _, pull_back = jax.vjp(rms_norm, activations, gain_row)
    return pull_back(gradient)


def heads_of(activations):
    return activations.reshape(activations.shape[0], HEADS, HDIM)


def logits_of(queries, keys_in, allowed):
    raw_logits = jnp.einsum(
        "qhd,khd->hqk", heads_of(queries), heads_of(keys_in), preferred_element_type=jnp.float32
    ) * HDIM ** (-0.5)
    if allowed is None:
        return raw_logits
    return jnp.where(allowed[None], raw_logits, -1e30)


def attend_forward(queries, keys_in, values, allowed):
    logits = logits_of(queries, keys_in, allowed)
    row_peak = jnp.max(logits, axis=-1, keepdims=True)
    weights = jnp.exp(logits - row_peak)
    row_total = jnp.sum(weights, axis=-1, keepdims=True)
    softmax_out = (weights / row_total).astype(jnp.bfloat16)
    mixed_heads = jnp.einsum(
        "hqk,khd->qhd", softmax_out, heads_of(values), preferred_element_type=jnp.float32
    )
    return (
        mixed_heads.reshape(queries.shape[0], D).astype(jnp.bfloat16),
        row_peak + jnp.log(row_total),
    )


def attend_backward(queries, keys_in, values, allowed, log_total, grad_mixed):
    softmax_out = jnp.exp(logits_of(queries, keys_in, allowed) - log_total)
    grad_heads = heads_of(grad_mixed)
    grad_softmax = jnp.einsum(
        "qhd,khd->hqk", grad_heads, heads_of(values), preferred_element_type=jnp.float32
    )
    grad_values = jnp.einsum(
        "hqk,qhd->khd",
        softmax_out.astype(jnp.bfloat16),
        grad_heads,
        preferred_element_type=jnp.float32,
    )
    inner_sum = jnp.sum(softmax_out * grad_softmax, axis=-1, keepdims=True)
    grad_logits = (softmax_out * (grad_softmax - inner_sum) * HDIM ** (-0.5)).astype(jnp.bfloat16)
    grad_queries = jnp.einsum(
        "hqk,khd->qhd", grad_logits, heads_of(keys_in), preferred_element_type=jnp.float32
    )
    grad_keys = jnp.einsum(
        "hqk,qhd->khd", grad_logits, heads_of(queries), preferred_element_type=jnp.float32
    )
    query_count = queries.shape[0]
    key_count = keys_in.shape[0]
    return (
        grad_queries.reshape(query_count, D),
        grad_keys.reshape(key_count, D),
        grad_values.reshape(key_count, D),
    )


def self_forward(inputs, gain_row, w_attn, allowed):
    normed = rms_norm(inputs, gain_row).astype(jnp.bfloat16)
    packed = project(normed, w_attn[:, : 3 * D]).astype(jnp.bfloat16)
    mixed_heads, log_total = attend_forward(
        packed[:, :D], packed[:, D : 2 * D], packed[:, 2 * D :], allowed
    )
    return (
        inputs + project(mixed_heads, w_attn[:, 3 * D :]),
        (normed, packed, mixed_heads, log_total),
    )


def self_backward(inputs, gain_row, w_attn, allowed, kept_values, grad_result):
    normed, packed, mixed_heads, log_total = kept_values
    grad_low = grad_result.astype(jnp.bfloat16)
    grad_proj = weight_grad(mixed_heads, grad_low)
    grad_mixed = input_back(grad_low, w_attn[:, 3 * D :]).astype(jnp.bfloat16)
    grad_queries, grad_keys, grad_values = attend_backward(
        packed[:, :D], packed[:, D : 2 * D], packed[:, 2 * D :], allowed, log_total, grad_mixed
    )
    grad_packed = jnp.concatenate([grad_queries, grad_keys, grad_values], axis=1).astype(
        jnp.bfloat16
    )
    grad_qkv = weight_grad(normed, grad_packed)
    grad_inputs, grad_gain = norm_back(
        inputs, gain_row, input_back(grad_packed, w_attn[:, : 3 * D])
    )
    return (grad_result + grad_inputs, grad_gain, jnp.concatenate([grad_qkv, grad_proj], axis=1))


def gated_unit(gated):
    return jax.nn.gelu(gated[:, :FF], approximate=True) * gated[:, FF:]


def ffn_forward(inputs, gain_row, w_in, w_out):
    normed = rms_norm(inputs, gain_row).astype(jnp.bfloat16)
    gated = project(normed, w_in)
    hidden = gated_unit(gated).astype(jnp.bfloat16)
    return (inputs + project(hidden, w_out), (normed, gated, hidden))


def ffn_backward(inputs, gain_row, w_in, w_out, kept_values, grad_result):
    normed, gated, hidden = kept_values
    grad_low = grad_result.astype(jnp.bfloat16)
    grad_wout = weight_grad(hidden, grad_low)
    _, pull_back = jax.vjp(gated_unit, gated)
    grad_gated = pull_back(input_back(grad_low, w_out))[0].astype(jnp.bfloat16)
    grad_win = weight_grad(normed, grad_gated)
    grad_inputs, grad_gain = norm_back(inputs, gain_row, input_back(grad_gated, w_in))
    return (grad_result + grad_inputs, grad_gain, grad_win, grad_wout)


def encoder_forward(inputs, weights):
    w_attn, w_extra, w_in, w_out, gain_rows = weights
    middle, first_kept = self_forward(inputs, gain_rows[0], w_attn, None)
    result, second_kept = ffn_forward(middle, gain_rows[1], w_in, w_out)
    normed = rms_norm(result, gain_rows[2]).astype(jnp.bfloat16)
    cross_kv = project(normed, w_extra).astype(jnp.bfloat16)
    return (result, cross_kv, (middle, first_kept, second_kept, normed))


def encoder_backward(inputs, weights, grad_result, grad_kv):
    w_attn, w_extra, w_in, w_out, gain_rows = weights
    result, _, kept_values = encoder_forward(inputs, weights)
    middle, first_kept, second_kept, normed = kept_values
    grad_extra = weight_grad(normed, grad_kv)
    grad_final, gain_final = norm_back(result, gain_rows[2], input_back(grad_kv, w_extra))
    grad_middle, gain_late, grad_win, grad_wout = ffn_backward(
        middle, gain_rows[1], w_in, w_out, second_kept, grad_result + grad_final
    )
    grad_inputs, gain_early, grad_attn = self_backward(
        inputs, gain_rows[0], w_attn, None, first_kept, grad_middle
    )
    return (
        grad_inputs,
        (
            grad_attn,
            grad_extra,
            grad_win,
            grad_wout,
            jnp.stack([gain_early, gain_late, gain_final]),
        ),
    )


def decoder_step(inputs, cross_kv, allowed, weights, grad_result):
    w_attn, w_extra, w_in, w_out, gain_rows = weights
    middle, first_kept = self_forward(inputs, gain_rows[0], w_attn, allowed)
    query_in = rms_norm(middle, gain_rows[2]).astype(jnp.bfloat16)
    queries = project(query_in, w_extra[:, :D]).astype(jnp.bfloat16)
    mixed_heads, log_total = attend_forward(queries, cross_kv[:, :D], cross_kv[:, D:], None)
    after_cross = middle + project(mixed_heads, w_extra[:, D:])
    result, second_kept = ffn_forward(after_cross, gain_rows[1], w_in, w_out)
    grad_after, gain_late, grad_win, grad_wout = ffn_backward(
        after_cross, gain_rows[1], w_in, w_out, second_kept, grad_result
    )
    grad_low = grad_after.astype(jnp.bfloat16)
    grad_cross_out = weight_grad(mixed_heads, grad_low)
    grad_mixed = input_back(grad_low, w_extra[:, D:]).astype(jnp.bfloat16)
    grad_queries, grad_keys, grad_values = attend_backward(
        queries, cross_kv[:, :D], cross_kv[:, D:], None, log_total, grad_mixed
    )
    grad_queries = grad_queries.astype(jnp.bfloat16)
    grad_cross_in = weight_grad(query_in, grad_queries)
    grad_normed, gain_cross = norm_back(
        middle, gain_rows[2], input_back(grad_queries, w_extra[:, :D])
    )
    grad_inputs, gain_early, grad_attn = self_backward(
        inputs, gain_rows[0], w_attn, allowed, first_kept, grad_after + grad_normed
    )
    grad_kv = jnp.concatenate([grad_keys, grad_values], axis=1).astype(jnp.bfloat16)
    gradients = (
        grad_attn,
        jnp.concatenate([grad_cross_in, grad_cross_out], axis=1),
        grad_win,
        grad_wout,
        jnp.stack([gain_early, gain_late, gain_cross]),
    )
    return (result, grad_inputs, grad_kv, gradients)


def local(acts, w_attn, w_extra, w_in, w_out, gains, segments, cotangent):
    gathered = (
        lax.all_gather(w_attn[0], "dp", axis=0, tiled=True),
        lax.all_gather(w_extra[0], "dp", axis=0, tiled=True),
        lax.all_gather(w_in[0], "dp", axis=0, tiled=True),
        lax.all_gather(w_out[0], "dp", axis=0, tiled=True),
        lax.all_gather(gains[0], "dp", axis=1, tiled=True),
    )
    weights = gathered[:4] + (gathered[4].astype(jnp.float32),)
    inputs = acts[0, :, 0]
    upstream = cotangent[0, :, 0]
    is_first = lax.axis_index("section") == 0
    positions = jnp.arange(SEQ)
    causal = positions[None, :] <= positions[:, None]
    zero_message = jnp.zeros((SEQ, 2 * D), jnp.bfloat16)
    zero_grads = tuple((jnp.zeros(weight.shape, jnp.float32) for weight in weights))
    carried = (jnp.zeros((MICRO, SEQ, D), jnp.float32), jnp.zeros((MICRO, SEQ, D), jnp.float32))
    received = zero_message
    returned = zero_message
    totals = zero_grads
    moments = MICRO + 2
    for moment in range(moments):

        def first_section(carried, received, returned):
            results, grad_inputs = carried
            message = zero_message
            fresh_grads = zero_grads
            if moment < MICRO:
                result, message, _ = encoder_forward(inputs[moment], weights)
                results = results.at[moment].set(result)
            if moment >= 2:
                grad_rows, fresh_grads = encoder_backward(
                    inputs[moment - 2], weights, upstream[moment - 2], returned
                )
                grad_inputs = grad_inputs.at[moment - 2].set(grad_rows)
            return ((results, grad_inputs), message, zero_message, fresh_grads)

        def second_section(carried, received, returned):
            results, grad_inputs = carried
            message = zero_message
            fresh_grads = zero_grads
            if 1 <= moment <= MICRO:
                segment_ids = segments[moment - 1, 0]
                allowed = (segment_ids[:, None] == segment_ids[None, :]) & causal
                result, grad_rows, message, fresh_grads = decoder_step(
                    inputs[moment - 1], received, allowed, weights, upstream[moment - 1]
                )
                results = results.at[moment - 1].set(result)
                grad_inputs = grad_inputs.at[moment - 1].set(grad_rows)
            return ((results, grad_inputs), zero_message, message, fresh_grads)

        carried, forward_message, back_message, fresh_grads = lax.cond(
            is_first, first_section, second_section, carried, received, returned
        )
        if moment < MICRO:
            received = from_behind(forward_message, "section", 1)
        if 1 <= moment <= MICRO:
            returned = from_behind(back_message, "section", -1)
        if moment >= 1:
            totals = tuple((jnp.add(*couple) for couple in zip(totals, fresh_grads)))
    results, grad_inputs = carried
    final = (
        lax.psum_scatter(totals[0], "dp", scatter_dimension=0, tiled=True),
        lax.psum_scatter(totals[1], "dp", scatter_dimension=0, tiled=True),
        lax.psum_scatter(totals[2], "dp", scatter_dimension=0, tiled=True),
        lax.psum_scatter(totals[3], "dp", scatter_dimension=0, tiled=True),
        lax.psum_scatter(totals[4], "dp", scatter_dimension=1, tiled=True),
    )
    return (
        results[None, :, None],
        grad_inputs[None, :, None],
        final[0][None],
        final[1][None],
        final[2][None],
        final[3][None],
        final[4][None],
    )


def solution(mesh):
    in_specs = (
        P("section", None, "dp", None, None),
        P("section", "dp", None),
        P("section", "dp", None),
        P("section", "dp", None),
        P("section", "dp", None),
        P("section", None, "dp"),
        P(None, "dp", None),
        P("section", None, "dp", None, None),
    )
    out_specs = (
        P("section", None, "dp", None, None),
        P("section", None, "dp", None, None),
        P("section", "dp", None),
        P("section", "dp", None),
        P("section", "dp", None),
        P("section", "dp", None),
        P("section", None, "dp"),
    )
    return jax.shard_map(local, mesh=mesh, in_specs=in_specs, out_specs=out_specs, check_vma=False)
```

profile of v0, /device:TPU:0, one launch (start us, length us, event | category | flops | bytes accessed | tf_op | source)
XLA Modules:
  0.0 1142.1 jit_solution(18382710055161982647)
XLA Ops:
  10.8 24.5 %all-gather = bf16[1,3,768]{1,0,2:T(2,128)(2,1)S(1)} all-gather(bf16[1,3,48]{1,0,2:T(2,128)(2,1)S(1)} %copy.218), channel_id=2, replica_groups=mesh['section'=2,'dp'=16] {'dp'}, dimensions={2}, use_global_device_ids=true | all-gather | bytes 4896 | tf_op jit(solution)/shard_map/all_gather | solution.py:229
  35.7 20.0 %all-gather.12.cloned.1.call-done = bf16[1,768,1536]{2,1,0:T(8,128)(2,1)} async-done(((bf16[1,48,1536]{2,1,0:T(8,128)(2,1)}), bf16[1,768,1536]{2,1,0:T(8,128)(2,1)}) %all-gather.12.cloned.1.call-update) | async-done | bytes 2359312 | tf_op jit(solution)/shard_map/all_gather | solution.py:226
  55.7 46.3 %all-gather.16.cloned.1.call-done = bf16[1,2048,768]{2,1,0:T(8,128)(2,1)} async-done(((bf16[1,128,768]{2,1,0:T(8,128)(2,1)}), bf16[1,2048,768]{2,1,0:T(8,128)(2,1)}) %all-gather.16.cloned.1.call-update) | async-done | bytes 3145744 | tf_op jit(solution)/shard_map/all_gather | solution.py:228
  102.0 54.5 %all-gather.10.cloned.1.call-done = bf16[1,768,3072]{2,1,0:T(8,128)(2,1)} async-done(((bf16[1,48,3072]{2,1,0:T(8,128)(2,1)}), bf16[1,768,3072]{2,1,0:T(8,128)(2,1)}) %all-gather.10.cloned.1.call-update) | async-done | bytes 4718608 | tf_op jit(solution)/shard_map/all_gather | solution.py:225
  156.5 62.6 %all-gather.14.cloned.1.call-done = bf16[1,768,4096]{2,1,0:T(8,128)(2,1)} async-done(((bf16[1,48,4096]{2,1,0:T(8,128)(2,1)}), bf16[1,768,4096]{2,1,0:T(8,128)(2,1)}) %all-gather.14.cloned.1.call-update) | async-done | bytes 6291472 | tf_op jit(solution)/shard_map/all_gather | solution.py:227
  219.1 20.4 %conditional.4 = (f32[2,256,768]{2,1,0:T(8,128)}, bf16[256,1536]{1,0:T(8,128)(2,1)S(1)}) conditional(s32[]{:T(128)} %convert_element_type.327, () %tuple.74, (f32[2,256,768]{2,1,0:T(8,128)}, f32[3,768]{0,1:T(8,128)S(1)}, bf16[768,3072]{1,0:T(8,128)(2,1)}, bf16[768,4096]{1,0:T(8,128)(2,1)}, bf16[2048,768]{1,0:T(8,128)(2,1)}, ...), branch_computations={%region_0.0_spmd, %region_1.7_spmd} | conditional | flops 4442883072 | bytes 95765656 | solution.py:274
  220.5 3.4 convolution_convert_fusion
  225.3 3.9 fusion.460
  241.7 16.8 %collective-permute-done = bf16[256,1536]{0,1:T(8,128)(2,1)S(1)} collective-permute-done((bf16[256,1536]{0,1:T(8,128)(2,1)S(1)}, bf16[256,1536]{0,1:T(8,128)(2,1)S(1)}, u32[]{:S(2)}, u32[]{:S(2)}) %collective-permute-start) | collective-permute-done | bytes 786464 | tf_op jit(solution)/shard_map/ppermute | solution.py:17
  258.5 47.1 %conditional.5 = (f32[2,256,768]{2,1,0:T(8,128)}, f32[2,256,768]{2,1,0:T(8,128)}, bf16[256,1536]{1,0:T(8,128)(2,1)S(1)}, bf16[256,1536]{0,1:T(8,128)(2,1)}, f32[...) conditional(s32[]{:T(128)} %convert_element_type.327, ...), branch_computations={%region_7.23_spmd, %region_23.29_spmd} | conditional | flops 13979039744 | bytes 431177408 | solution.py:274
  267.7 3.4 convolution_convert_fusion.6
  272.4 4.0 fusion.465
  291.7 3.0 broadcast_in_dim.124
  294.7 4.8 broadcast_in_dim.121
  299.5 6.0 broadcast_in_dim.123
  306.8 87.6 %collective-permute-start.1 = (bf16[256,1536]{0,1:T(8,128)(2,1)}, bf16[256,1536]{0,1:T(8,128)(2,1)S(1)}, u32[]{:S(2)}, u32[]{:S(2)}) collective-permute-start(bf16[256,1536]{0,1:T(8,128)(2,1)} %copy.223), channel_id=1, source_target_pairs={{0,16},{1,17},{2,18},{3,19},{4,20},{5,21},{6,22},{7,23},{8,24},{9,... | collective-permute-start | bytes 2359304 | tf_op jit(solution)/shard_map/ppermute | solution.py:17
  397.0 14.3 %collective-permute-done.1 = bf16[256,1536]{0,1:T(8,128)(2,1)S(1)} collective-permute-done((bf16[256,1536]{0,1:T(8,128)(2,1)}, bf16[256,1536]{0,1:T(8,128)(2,1)S(1)}, u32[]{:S(2)}, u32[]{:S(2)}) %collective-permute-start.1) | collective-permute-done | bytes 786464 | tf_op jit(solution)/shard_map/ppermute | solution.py:17
  411.3 5.4 collective-permute-done.2
  416.7 94.7 %conditional.6 = (f32[2,256,768]{2,1,0:T(8,128)}, bf16[256,1536]{0,1:T(8,128)(2,1)}, f32[768,3072]{1,0:T(8,128)}, f32[768,4096]{1,0:T(8,128)}, f32[2048,768]{1,0...) conditional(s32[]{:T(128)} %convert_element_type.327, ...), branch_computations={%region_29.45_spmd, %region_45.58_spmd} | conditional | flops 13979039744 | bytes 413352576 | solution.py:274
  426.6 3.1 convolution_convert_fusion.12
  453.7 3.5 fusion.343
  461.4 7.2 fusion.336
  468.6 7.2 fusion.339
  475.7 3.5 multiply_reduce_fusion.30
  480.5 4.3 fusion.357
  484.9 3.8 fusion.365
  488.7 4.2 fusion.356
  492.9 8.7 pad_maximum_fusion.14
  501.5 8.7 fusion.360
  514.7 62.4 %collective-permute-done.3 = bf16[256,1536]{1,0:T(8,128)(2,1)} collective-permute-done((bf16[256,1536]{1,0:T(8,128)(2,1)S(1)}, bf16[256,1536]{1,0:T(8,128)(2,1)}, u32[]{:S(2)}, u32[]{:S(2)}) %collective-permute-start.3) | collective-permute-done | bytes 786464 | tf_op jit(solution)/shard_map/ppermute | solution.py:17
  577.1 79.8 %conditional.7 = (f32[2,256,768]{2,1,0:T(8,128)}, f32[768,3072]{1,0:T(8,128)}, f32[768,1536]{1,0:T(8,128)}, f32[768,4096]{1,0:T(8,128)}, f32[2048,768]{1,0:T(8,128)}, /*index=5*/f32[3,768]{1,0:T(4,128)S(1)}) conditional(s32[]{:T(128)} %convert_element_type.327, f32[2,256,768]{2,1,0:T(8,128)} %get-tuple-element.302, (f32[2,256,768]{2,1,0:T(8,128)}, ...), branch_computations={%region_58.0_spmd, %region_59.72_spmd} | conditional | flops 12751546368 | bytes 328581312 | solution.py:274
  578.5 3.1 convolution_convert_fusion.14
  609.9 7.1 fusion.410
  617.0 7.1 fusion.413
  624.1 3.3 multiply_reduce_fusion.39
  629.2 4.3 fusion.431
  633.5 3.7 fusion.439
  637.2 4.1 fusion.430
  641.3 8.9 pad_maximum_fusion.19
  650.2 6.4 fusion.434
  658.7 8.9 add_add_fusion.15
  667.6 10.5 add_add_fusion.14
  678.2 14.8 %add_add_fusion.13 = f32[768,3072]{1,0:T(8,128)} fusion(f32[768,3072]{1,0:T(8,128)} %get-tuple-element.307, f32[768,3072]{1,0:T(8,128)} %get-tuple-element.305, f32[768,3072]{1,0:T(8,128)} %get-tuple-element.306), kind=kLoop, calls=%fused_computation.613 | loop fusion | flops 4718592 | bytes 37748736 | tf_op jit(solution)/shard_map/add | solution.py:282
  693.1 18.3 %add_add_fusion.12 = f32[768,4096]{1,0:T(8,128)} fusion(f32[768,4096]{1,0:T(8,128)} %get-tuple-element.313, f32[768,4096]{1,0:T(8,128)} %get-tuple-element.311, f32[768,4096]{1,0:T(8,128)} %get-tuple-element.312), kind=kLoop, calls=%fused_computation.612 | loop fusion | flops 6291456 | bytes 50331648 | tf_op jit(solution)/shard_map/add | solution.py:282
  713.4 78.0 %reduce-scatter.10.cloned.1.call-done = f32[48,1536]{1,0:T(8,128)} async-done(((f32[768,1536]{1,0:T(8,128)}), f32[48,1536]{1,0:T(8,128)}) %reduce-scatter.10.cloned.1.call-update) | async-done | bytes 294928 | tf_op jit(solution)/shard_map/reduce_scatter | solution.py:286
  791.5 88.8 %reduce-scatter.14.cloned.1.call-done = f32[128,768]{1,0:T(8,128)} async-done(((f32[2048,768]{1,0:T(8,128)}), f32[128,768]{1,0:T(8,128)}) %reduce-scatter.14.cloned.1.call-update) | async-done | bytes 393232 | tf_op jit(solution)/shard_map/reduce_scatter | solution.py:288
  880.3 115.7 %reduce-scatter.8.cloned.1.call-done = f32[48,3072]{1,0:T(8,128)} async-done(((f32[768,3072]{1,0:T(8,128)}), f32[48,3072]{1,0:T(8,128)}) %reduce-scatter.8.cloned.1.call-update) | async-done | bytes 589840 | tf_op jit(solution)/shard_map/reduce_scatter | solution.py:285
  996.0 139.0 %reduce-scatter.12.cloned.1.call-done = f32[48,4096]{1,0:T(8,128)} async-done(((f32[768,4096]{1,0:T(8,128)}), f32[48,4096]{1,0:T(8,128)}) %reduce-scatter.12.cloned.1.call-update) | async-done | bytes 786448 | tf_op jit(solution)/shard_map/reduce_scatter | solution.py:287
  (317 shorter events, 110.6 us)
Async XLA Ops:
  7.2 48.5 %all-gather.12.cloned.1.call-start = ((), (), s32[]{:S(2)}) async-start(), calls=%async_computation.10 | async-start | bytes 2506752 | tf_op jit(solution)/shard_map/all_gather | solution.py:226
  7.9 94.1 %all-gather.16.cloned.1.call-start = ((), (), s32[]{:S(2)}) async-start(), calls=%async_computation.12 | async-start | bytes 3342336 | tf_op jit(solution)/shard_map/all_gather | solution.py:228
  8.6 147.8 %all-gather.10.cloned.1.call-start = ((), (), s32[]{:S(2)}) async-start(), calls=%async_computation.9 | async-start | bytes 5013504 | tf_op jit(solution)/shard_map/all_gather | solution.py:225
  9.4 209.7 %all-gather.14.cloned.1.call-start = ((), (), s32[]{:S(2)}) async-start(), calls=%async_computation.11 | async-start | bytes 6684672 | tf_op jit(solution)/shard_map/all_gather | solution.py:227
  10.0 702.1 %reduce-scatter.16.cloned.1.call-start = ((), (), s32[]{:S(2)}) async-start(), calls=%async_computation.13 | async-start | bytes 417792
  219.0 39.4 %copy-start.165 = (s32[2,1,256]{2,1,0:T(1,128)S(1)}, s32[2,1,256]{2,1,0:T(1,128)}, u32[]{:S(2)}) copy-start(s32[2,1,256]{2,1,0:T(1,128)} %param.38) | copy-start | bytes 6148
  225.3 8.5 slice-start
  229.2 4.5 slice-start.1
  239.7 18.8 %collective-permute-start = (bf16[256,1536]{0,1:T(8,128)(2,1)S(1)}, bf16[256,1536]{0,1:T(8,128)(2,1)S(1)}, u32[]{:S(2)}, u32[]{:S(2)}) collective-permute-start(bf16[256,1536]{0,1:T(8,128)(2,1)S(1)} %copy.220), channel_id=1, source_target_pairs={{0,16},{1,17},{2,18},{3,19},{4,20},{5,21},{6,22},{7,23},{8,24},{9,... | collective-permute-start | bytes 2359304 | tf_op jit(solution)/shard_map/ppermute | solution.py:17
  272.4 8.5 slice-start.4
  276.4 4.5 slice-start.5
  305.6 111.1 %copy-start = (f32[1,2,1,256,768]{4,3,2,1,0:T(8,128)S(1)}, f32[1,2,1,256,768]{4,3,2,1,0:T(8,128)}, u32[]{:S(2)}) copy-start(f32[1,2,1,256,768]{4,3,2,1,0:T(8,128)} %param.32) | copy-start | bytes 4718596
  305.6 111.1 %copy-start.166 = (s32[2,1,256]{2,1,0:T(1,128)S(1)}, s32[2,1,256]{2,1,0:T(1,128)}, u32[]{:S(2)}) copy-start(s32[2,1,256]{2,1,0:T(1,128)} %param.38) | copy-start | bytes 6148
  306.8 104.5 %collective-permute-start.1 = (bf16[256,1536]{0,1:T(8,128)(2,1)}, bf16[256,1536]{0,1:T(8,128)(2,1)S(1)}, u32[]{:S(2)}, u32[]{:S(2)}) collective-permute-start(bf16[256,1536]{0,1:T(8,128)(2,1)} %copy.223), channel_id=1, source_target_pairs={{0,16},{1,17},{2,18},{3,19},{4,20},{5,21},{6,22},{7,23},{8,24},{9,... | collective-permute-start | bytes 2359304 | tf_op jit(solution)/shard_map/ppermute | solution.py:17
  395.7 20.9 %collective-permute-start.2 = (bf16[256,1536]{1,0:T(8,128)(2,1)S(1)}, bf16[256,1536]{1,0:T(8,128)(2,1)}, u32[]{:S(2)}, u32[]{:S(2)}) collective-permute-start(bf16[256,1536]{1,0:T(8,128)(2,1)S(1)} %copy.224), channel_id=1, source_target_pairs={{16,0},{17,1},{18,2},{19,3},{20,4},{21,5},{22,6},{23,7},{24,8},{25... | collective-permute-start | bytes 2359304 | tf_op jit(solution)/shard_map/ppermute | solution.py:17
  431.0 5.4 slice-start.8
  432.2 4.3 slice-start.9
  433.0 5.4 copy-start.117
  440.2 4.1 copy-start.44
  441.4 3.8 copy-start.48
  445.2 4.7 copy-start.32
  453.7 5.4 copy-start.56
  453.7 5.4 copy-start.92
  480.5 4.3 copy-start.33
  480.5 4.3 copy-start.45
  484.8 3.8 copy-start.74
  484.8 3.8 copy-start.107
  484.8 3.8 copy-start.109
  513.4 63.7 %collective-permute-start.3 = (bf16[256,1536]{1,0:T(8,128)(2,1)S(1)}, bf16[256,1536]{1,0:T(8,128)(2,1)}, u32[]{:S(2)}, u32[]{:S(2)}) collective-permute-start(bf16[256,1536]{1,0:T(8,128)(2,1)S(1)} %copy.227), channel_id=1, source_target_pairs={{16,0},{17,1},{18,2},{19,3},{20,4},{21,5},{22,6},{23,7},{24,8},{25... | collective-permute-start | bytes 2359304 | tf_op jit(solution)/shard_map/ppermute | solution.py:17
  582.9 5.4 slice-start.10
  584.1 4.3 slice-start.11
  584.9 5.4 copy-start.119
  588.3 13.6 %copy-start.30 = (f32[256,768]{1,0:T(8,128)}, f32[256,768]{1,0:T(8,128)S(1)}, u32[]{:S(2)}) copy-start(f32[256,768]{1,0:T(8,128)S(1)} %get-tuple-element.528) | copy-start | bytes 2359300 | tf_op jit(solution)/shard_map/cond
  592.2 4.1 copy-start.46
  597.2 4.7 copy-start.34
  603.1 4.6 copy-start.94
  609.9 7.1 copy-start.90
  617.0 7.1 copy-start.108
  629.2 4.3 copy-start.35
  629.2 4.3 copy-start.47
  641.3 8.9 copy-start.31
  641.3 8.9 copy-start.69
  641.3 8.9 copy-start.71
  650.2 6.4 copy-start.127
  658.6 132.8 %reduce-scatter.10.cloned.1.call-start = ((), (), s32[]{:S(2)}) async-start(), calls=%async_computation.6 | async-start | bytes 5013504 | tf_op jit(solution)/shard_map/reduce_scatter | solution.py:286
  667.6 212.7 %reduce-scatter.14.cloned.1.call-start = ((), (), s32[]{:S(2)}) async-start(), calls=%async_computation.8 | async-start | bytes 6684672 | tf_op jit(solution)/shard_map/reduce_scatter | solution.py:288
  678.1 317.9 %reduce-scatter.8.cloned.1.call-start = ((), (), s32[]{:S(2)}) async-start(), calls=%async_computation.5 | async-start | bytes 10027008 | tf_op jit(solution)/shard_map/reduce_scatter | solution.py:285
  693.0 442.1 %reduce-scatter.12.cloned.1.call-start = ((), (), s32[]{:S(2)}) async-start(), calls=%async_computation.7 | async-start | bytes 13369344 | tf_op jit(solution)/shard_map/reduce_scatter | solution.py:287
  (50 other events, 108.6 us)
Sparse Core Ops, SparseCore 0:
  10.3 45.3 all-gather.11
  57.9 43.9 all-gather.15
  104.2 52.1 all-gather.9
  158.6 60.3 all-gather.13
  658.7 53.2 reduce-scatter.15
  716.8 74.5 reduce-scatter.9
  796.0 84.2 reduce-scatter.13
  885.5 110.4 reduce-scatter.7
  1000.7 134.3 reduce-scatter.11
where the time goes:
time: 1150 us; the launch traced here: 1140 us
  waiting for transfers between devices  707 us (61%)
  matrix products  153 us (13%)
  starting transfers between devices  91.8 us (8%)
  other arithmetic  82.3 us (7%)
  local copies, waits for them, and re-layouts  51.1 us (4%)
  blocking collectives  24.5 us (2%)
  loops' own time  18 us (2%)
  between operations  14.4 us (1%)
    reduce_scatter x1, waiting for transfers between devices, local(): lax.psum_scatter(totals[2], 'dp', scatter_dimension=0, tiled=True)  139 us
    reduce_scatter x1, waiting for transfers between devices, local(): lax.psum_scatter(totals[0], 'dp', scatter_dimension=0, tiled=True)  116 us
    ppermute x4, waiting for transfers between devices, from_behind(): return lax.ppermute(block, axis, route)  98.8 us
    ppermute x4, starting transfers between devices, from_behind(): return lax.ppermute(block, axis, route)  91.5 us
    reduce_scatter x1, waiting for transfers between devices, local(): lax.psum_scatter(totals[3], 'dp', scatter_dimension=0, tiled=True)  88.8 us
    reduce_scatter x1, waiting for transfers between devices, local(): lax.psum_scatter(totals[1], 'dp', scatter_dimension=0, tiled=True)  78 us
    all_gather x1, waiting for transfers between devices, local(): lax.all_gather(w_in[0], 'dp', axis=0, tiled=True)  62.6 us
    all_gather x1, waiting for transfers between devices, local(): lax.all_gather(w_attn[0], 'dp', axis=0, tiled=True)  54.5 us
  transfers between devices with their start and end apart: 13, of which 13 were waited for; matrix products, arithmetic and copies ran while one was open for 5% of the time, Pallas kernels for 0%

commit v1 on v0

--- a/solution.py
+++ b/solution.py
@@ -1,14 +1,852 @@
 import jax
 import jax.numpy as jnp
 from jax import lax
+from jax.experimental import pallas as pl
+from jax.experimental.pallas import tpu as pltpu
 from jax.sharding import PartitionSpec as P
 
-D = 768
-HEADS = 12
-HDIM = 64
-FF = 2048
-SEQ = 256
-MICRO = 2
+D=768; HEADS=12; HDIM=64; FF=2048; SEQ=256; MICRO=2
+ROWS=MICRO*SEQ
+BF=jnp.bfloat16; F32=jnp.float32
+QKV, OP, XA, XB, WIN, KV = 0, 3*D, 4*D, 5*D, 6*D, 6*D+2*FF
+WIDE = KV + 2*D
+NN=(((1,),(0,)),((),())); NT=(((1,),(1,)),((),()))
+
+def mul(start, k): return pl.multiple_of(start, k)
+def dot(a,b,dims=NN): return lax.dot_general(a,b,dims,preferred_element_type=F32)
+
+def wide_cols(wa, start, size):
+    return wa[:, :, :, :, pl.ds(start, size)].reshape(D, size)
+
+def rms_rows(v):
+    return lax.rsqrt(jnp.mean(v*v, axis=-1, keepdims=True) + 1e-6)
+
+def norm_forward(v_ref, gain, n_ref, first=0, count=ROWS):
+    @pl.loop(0, count//64)
+    def _(i):
+        rows=pl.ds(mul(first+i*64,64),64)
+        v=v_ref[rows,:]
+        n_ref[rows,:]=(v*rms_rows(v)*gain).astype(BF)
+
+def norm_backward(v_ref, gain, dn_ref, g_ref, dgain_ref, slot, first=0, count=ROWS):
+    def body(i, acc):
+        rows=pl.ds(mul(first+i*64,64),64)
+        v=v_ref[rows,:]; dn=dn_ref[rows,:]
+        r=rms_rows(v)
+        t=dn*gain
+        vr=v*r
+        g_ref[rows,:]+= r*(t - vr*jnp.mean(t*vr,axis=-1,keepdims=True))
+        return acc+jnp.sum(dn*vr,axis=0,keepdims=True)
+    acc=lax.fori_loop(0,count//64,body,jnp.zeros((1,D),F32))
+    dgain_ref[slot:slot+1,:]+=acc
+
+def transpose_to(src_ref, dst_ref, first=0, count=ROWS):
+    cols=src_ref.shape[1]
+    @pl.loop(0, cols//128)
+    def _(j):
+        cs=pl.ds(mul(j*128,128),128)
+        dst_ref[cs, pl.ds(first,count)] = src_ref[pl.ds(first,count),cs].T
+
+def project(n_ref, wa, wcol, out_ref, ocol, total, tile, first=0, count=ROWS):
+    @pl.loop(0, total//tile)
+    def _(j):
+        w=wide_cols(wa, mul(wcol+j*tile,128), tile)
+        out_ref[pl.ds(first,count), pl.ds(mul(ocol+j*tile,128),tile)] = dot(n_ref[pl.ds(first,count),:], w).astype(out_ref.dtype)
+
+def project_add(a_ref, wa, wcol, base_ref, out_ref, tile, first=0, count=ROWS):
+    rows=pl.ds(first,count)
+    @pl.loop(0, D//tile)
+    def _(j):
+        w=wide_cols(wa, mul(wcol+j*tile,128), tile)
+        cs=pl.ds(mul(j*tile,128),tile)
+        out_ref[rows,cs] = base_ref[rows,cs]+dot(a_ref[rows,:], w)
+
+def back_project(g_ref, gcol, wa, wcol, total, tile, acc_ref, first=0, count=ROWS, fresh=True):
+    rows=pl.ds(first,count)
+    def part(j):
+        w=wide_cols(wa, mul(wcol+j*tile,128), tile)
+        return dot(g_ref[rows, pl.ds(mul(gcol+j*tile,128),tile)], w, NT)
+    if fresh:
+        acc_ref[rows,:]=part(0)
+    @pl.loop(1 if fresh else 0, total//tile)
+    def _(j):
+        acc_ref[rows,:]+=part(j)
+
+def attend_forward(q_ref, qc, k_ref, kc, v_ref, vc, o_ref, oT_ref, mask_ref, start, stop):
+    @pl.loop(start, stop)
+    def _(i):
+        img=i//6; p=i%6
+        rows=pl.ds(mul(img*SEQ,SEQ),SEQ)
+        def cols(base): return pl.ds(mul(base+p*128,128),128)
+        q2=q_ref[rows,cols(qc)]*jnp.asarray(0.125,BF)
+        k2=k_ref[rows,cols(kc)]
+        vT=v_ref[rows,cols(vc)].T
+        lane=lax.broadcasted_iota(jnp.int32,(SEQ,128),1)//64
+        parts=[]
+        for a in range(2):
+            ka=jnp.where(lane==a,k2,jnp.zeros_like(k2))
+            s=dot(ka,q2,NT)
+            if mask_ref is not None:
+                s=jnp.where(mask_ref[img].astype(F32)>0,s,-1e30)
+            e=jnp.exp(s-jnp.max(s,axis=0,keepdims=True))
+            w=(e*(1.0/jnp.sum(e,axis=0,keepdims=True))).astype(BF)
+            parts.append(dot(vT[a*64:(a+1)*64],w))
+        oT=jnp.concatenate(parts,axis=0).astype(BF)
+        oT_ref[pl.ds(mul(p*128,128),128),rows]=oT
+        o_ref[rows,cols(0)]=oT.T
+
+def attend_backward(q_ref, qc, k_ref, kc, v_ref, vc, d_ref, mask_ref, dq_ref, dqc, dk_ref, dkc, dv_ref, dvc, start, stop):
+    @pl.loop(start, stop)
+    def _(i):
+        img=i//6; p=i%6
+        rows=pl.ds(mul(img*SEQ,SEQ),SEQ)
+        def cols(base): return pl.ds(mul(base+p*128,128),128)
+        q2=q_ref[rows,cols(qc)]
+        qs=q2*jnp.asarray(0.125,BF)
+        k2=k_ref[rows,cols(kc)]
+        v2=v_ref[rows,cols(vc)]
+        d2=d_ref[rows,cols(0)]
+        kT=k2.T
+        lane=lax.broadcasted_iota(jnp.int32,(SEQ,128),1)//64
+        dqT=[]; dk=[]; dv=[]
+        for a in range(2):
+            mine=lane==a
+            s=dot(jnp.where(mine,k2,jnp.zeros_like(k2)),qs,NT)
+            if mask_ref is not None:
+                s=jnp.where(mask_ref[img].astype(F32)>0,s,-1e30)
+            e=jnp.exp(s-jnp.max(s,axis=0,keepdims=True))
+            w=e*(1.0/jnp.sum(e,axis=0,keepdims=True))
+            dw=dot(jnp.where(mine,v2,jnp.zeros_like(v2)),d2,NT)
+            wd=w*dw
+            ds=((wd-w*jnp.sum(wd,axis=0,keepdims=True))*0.125).astype(BF)
+            dv.append(dot(w.astype(BF),d2))
+            dk.append(dot(ds,q2))
+            dqT.append(dot(kT[a*64:(a+1)*64],ds))
+        dq_ref[rows,cols(dqc)]=jnp.concatenate(dqT,axis=0).astype(BF).T
+        dk_ref[rows,cols(dkc)]=jnp.where(lane==0,dk[0],dk[1]).astype(BF)
+        dv_ref[rows,cols(dvc)]=jnp.where(lane==0,dv[0],dv[1]).astype(BF)
+
+C0=0.7978845608028654; C1=0.044715
+def gated_forward(n_ref, wa, gu_ref, hid_ref, start, stop, first=0, count=ROWS, tile=256):
+    rows=pl.ds(first,count)
+    @pl.loop(start, stop)
+    def _(j):
+        lo=pl.ds(mul(j*tile,tile),tile); hi=pl.ds(mul(FF+j*tile,tile),tile)
+        gate=dot(n_ref[rows,:], wide_cols(wa, mul(WIN+j*tile,128), tile))
+        up=dot(n_ref[rows,:], wide_cols(wa, mul(WIN+FF+j*tile,128), tile))
+        t=jnp.tanh(C0*(gate+C1*gate*gate*gate))
+        hid_ref[rows,lo]=((0.5*gate*(1.0+t))*up).astype(BF)
+        gu_ref[rows,lo]=gate.astype(BF)
+        gu_ref[rows,hi]=up.astype(BF)
+
+def down_forward(hid_ref, wo, base_ref, out_ref, first=0, count=ROWS):
+    rows=pl.ds(first,count)
+    def part(j):
+        return dot(hid_ref[rows,pl.ds(mul(j*256,256),256)], wo[j//2,j%2].reshape(256,D))
+    out_ref[rows,:]=base_ref[rows,:]+part(0)
+    @pl.loop(1, FF//256)
+    def _(j):
+        out_ref[rows,:]+=part(j)
+
+def gated_backward(gb_ref, wo, gu_ref, start, stop, first=0, count=ROWS, tile=256):
+    rows=pl.ds(first,count)
+    @pl.loop(start, stop)
+    def _(j):
+        lo=pl.ds(mul(j*tile,tile),tile); hi=pl.ds(mul(FF+j*tile,tile),tile)
+        dh=dot(gb_ref[rows,:], wo[j//2,j%2].reshape(256,D), NT)
+        gate=gu_ref[rows,lo].astype(F32); up=gu_ref[rows,hi].astype(F32)
+        sq=gate*gate
+        t=jnp.tanh(C0*(gate+C1*gate*sq))
+        h=0.5*(1.0+t)
+        slope=h+0.5*gate*(1.0-t*t)*(C0+(3*C0*C1)*sq)
+        gu_ref[rows,lo]=(dh*up*slope).astype(BF)
+        gu_ref[rows,hi]=(dh*(gate*h)).astype(BF)
+
+def half_rows(nT_ref, c):
+    return jnp.concatenate([nT_ref[pl.ds(mul((2*j+c)*48,16),48),:] for j in range(8)],axis=0)
+
+
+MESH = pl.DeviceIdType.MESH
+BIG = 1152
+
+LINE = (
+    ("attn", 0, "wide", QKV, 1152),
+    ("attn", 1152, "wide", QKV + 1152, 1152),
+    ("attn", 3 * D, "wide", OP, D),
+    ("in", 0, "wide", WIN, 1024),
+    ("in", FF, "wide", WIN + FF, 1024),
+    ("in", 1024, "wide", WIN + 1024, 1024),
+    ("in", FF + 1024, "wide", WIN + FF + 1024, 1024),
+    ("out", 0, "tall", 0, 384),
+    ("out", 384, "tall", 384, 384),
+)
+PAIR = (("extra", 0, 512), ("extra", 512, 512), ("extra", 1024, 512))
+SUMS = {
+    "out0": ("tall", 0, 384), "out1": ("tall", 384, 384),
+    "in0": ("wide", WIN, 1024), "in1": ("wide", WIN + 1024, 1024),
+    "in2": ("wide", WIN + FF, 1024), "in3": ("wide", WIN + FF + 1024, 1024),
+    "x0": ("wide", XA, D), "x1": ("wide", XB, D),
+    "k0": ("wide", KV, D), "k1": ("wide", KV + D, D),
+    "o": ("wide", OP, D),
+    "q0": ("wide", QKV, 1152), "q1": ("wide", QKV + 1152, 1152),
+}
+SUM_NAMES = tuple(SUMS)
+OUT_OF = {
+    "out0": ("out", 0), "out1": ("out", 384), "in0": ("in", 0), "in1": ("in", 1024), "in2": ("in", FF), "in3": ("in", FF + 1024),
+    "x0": ("extra", 0), "x1": ("extra", D), "o": ("attn", 3 * D), "q0": ("attn", 0), "q1": ("attn", 1152),
+}
+FREE = {"out": 0, "in": 1, "x": 2, "k": 3, "o": 4, "q": 5}
+
+
+def scratch_list():
+    V, DMA, REG = pltpu.VMEM, pltpu.SemaphoreType.DMA, pltpu.SemaphoreType.REGULAR
+    n, m, s = len(LINE), len(PAIR), len(SUMS)
+    return dict(
+        wide=V((4, 2, 2, 48, WIDE), BF), tall=V((4, 2, 2, 128, D), BF),
+        y_wide=V((4, 48, WIDE), BF), y_tall=V((4, 128, D), BF),
+        z_wide=V((3, 48, WIDE), BF), z_tall=V((3, 128, D), BF),
+        stage=V((2, 4, 2, 48, BIG), BF), stage_tall=V((4, 2, 128, D), BF),
+        fin=V((2, 48, BIG), F32), fin_tall=V((2, 128, 384), F32),
+        x=V((ROWS, D), F32), mid=V((ROWS, D), F32), late=V((ROWS, D), F32), g=V((ROWS, D), F32), acc=V((ROWS, D), F32),
+        n1=V((ROWS, D), BF), n2=V((ROWS, D), BF), n3=V((ROWS, D), BF), xin=V((ROWS, D), BF), nT=V((D, ROWS), BF),
+        qkv=V((ROWS, 3 * D), BF), ao=V((ROWS, D), BF), aoT=V((D, ROWS), BF),
+        xq=V((ROWS, D), BF), kv=V((ROWS, 2 * D), BF), cm=V((ROWS, D), BF), cmT=V((D, ROWS), BF),
+        gu=V((ROWS, 2 * FF), BF), hid=V((ROWS, FF), BF), gb=V((ROWS, D), BF),
+        mask=V((MICRO, SEQ, SEQ), BF), xsend=V((ROWS, D), BF),
+        gz=V((4, 8, D), F32), gy=V((2, 8, D), F32), gc=V((2, 8, D), F32), gain=V((8, D), F32),
+        dgain=V((8, D), F32), hz=V((4, 8, D), F32), hy=V((2, 8, D), F32), hc=V((2, 8, D), F32),
+        s_in=DMA((4,)), s_own=DMA((n + m,)),
+        s_rs=DMA((n + m, 3)), s_rr=DMA((n + m, 3)), s_ls=DMA((n + m, 3)), s_lr=DMA((n + m, 3)),
+        s_ys=DMA((n + m, 4)), s_yr=DMA((n + m, 4)), s_cs=DMA((n + 2 * m,)), s_cr=DMA((n + 2 * m,)),
+        s_xs=DMA((m,)), s_xr=DMA((m,)), s_ms=DMA((MICRO,)), s_mr=DMA((MICRO,)),
+        s_gs=DMA((2, 5)), s_gr=DMA((2, 5)),
+        t_cs=DMA((s,)), t_cr=DMA((s,)), t_ys=DMA((s,)), t_yr=DMA((s,)), t_zs=DMA((s, 3)), t_zr=DMA((s, 3)),
+        t_xs=DMA((2,)), t_xr=DMA((2,)), t_out=DMA((s,)), s_out=DMA((3,)),
+        free=REG((len(FREE),)),
+    )
+
+
+def whole_kernel(*refs):
+    (acts_h, cot_h, attn_h, extra_h, in_h, out_h, gain_in, seg_in) = refs[:8]
+    (res_o, grad_o, attn_o, extra_o, gin_o, gout_o, gain_o) = refs[8:15]
+    R = type("Refs", (), {})()
+    for name, ref in zip(scratch_list(), refs[15:]):
+        setattr(R, name, ref)
+    src = {"attn": attn_h, "extra": extra_h, "in": in_h, "out": out_h}
+    dst = {"attn": attn_o, "extra": extra_o, "in": gin_o, "out": gout_o}
+    buf = {"wide": R.wide, "tall": R.tall}
+    ybuf = {"wide": R.y_wide, "tall": R.y_tall}
+    zbuf = {"wide": R.z_wide, "tall": R.z_tall}
+
+    section = lax.axis_index("section")
+    me = lax.axis_index("dp")
+    z, y, c = me // 4, (me // 2) % 2, me % 2
+    first, second = section == 0, section == 1
+    at = lambda zz, yy, cc: {"dp": zz * 4 + yy * 2 + cc}
+    right, left = at(lax.rem(z + 1, 4), y, c), at(lax.rem(z + 3, 4), y, c)
+    z_peer = [at(lax.rem(z + k, 4), y, c) for k in (1, 2, 3)]
+    y_peer, c_peer, x_peer = at(z, 1 - y, c), at(z, y, 1 - c), {"section": 1 - section}
+
+    def remote(a, b, ss, rs, dev):
+        return pltpu.make_async_remote_copy(a, b, ss, rs, device_id=dev, device_id_type=MESH)
+
+    def local(a, b, s):
+        return pltpu.make_async_copy(a, b, s)
+
+    def when(cond, fn):
+        pl.when(cond)(fn)
+
+    barrier = pltpu.get_barrier_semaphore()
+    everyone = z_peer + [y_peer, c_peer, x_peer]
+    for peer in everyone:
+        pl.semaphore_signal(barrier, inc=1, device_id=peer, device_id_type=MESH)
+    pl.semaphore_wait(barrier, len(everyone))
+
+    n, m = len(LINE), len(PAIR)
+    xoff = jnp.where(first, KV, XA)
+
+    def spot(i):
+        if i < n:
+            arg, lo, name, col, size = LINE[i]
+            return buf[name], pl.ds(col, size), src[arg].at[:, pl.ds(lo, size)]
+        arg, lo, size = PAIR[i - n]
+        return R.wide, pl.ds(mul(xoff + lo, 128), size), src[arg].at[:, pl.ds(lo, size)]
+
+    def own_copy(i):
+        b, cs, h = spot(i)
+        return local(h, b.at[z, y, c, :, cs], R.s_own.at[i])
+
+    def line_block(i, zz):
+        b, cs, h = spot(i)
+        return b.at[zz, y, c, :, cs] if i < n else b.at[zz, :, c, :, cs]
+
+    def go_right(i, s):
+        _, _, h = spot(i)
+        d = line_block(i, z - s)
+        return remote(h if s == 0 and i < n else d, d, R.s_rs.at[i, s], R.s_rr.at[i, s], right)
+
+    def go_left(i, s):
+        _, _, h = spot(i)
+        d = line_block(i, z + s)
+        return remote(h if s == 0 and i < n else d, d, R.s_ls.at[i, s], R.s_lr.at[i, s], left)
+
+    def from_left(i, s):
+        d = line_block(i, z - s)
+        return remote(d, d, R.s_rs.at[i, s - 1], R.s_rr.at[i, s - 1], left)
+
+    def from_right(i, s):
+        d = line_block(i, z + s)
+        return remote(d, d, R.s_ls.at[i, s - 1], R.s_lr.at[i, s - 1], right)
+
+    def across(i, zz, own=False):
+        b, cs, h = spot(i)
+        d = b.at[zz, y, c, :, cs]
+        return remote(h if own else d, d, R.s_ys.at[i, zz if i < n else 0], R.s_yr.at[i, zz if i < n else 0], y_peer)
+
+    def across_in(i, zz):
+        b, cs, h = spot(i)
+        d = b.at[zz, 1 - y, c, :, cs]
+        k = zz if i < n else 0
+        return remote(d, d, R.s_ys.at[i, k], R.s_yr.at[i, k], y_peer)
+
+    def core_in(i):
+        b, cs, h = spot(i)
+        d = b.at[:, :, 1 - c, :, cs]
+        return remote(d, d, R.s_cs.at[i], R.s_cr.at[i], c_peer)
+
+    def to_core(i):
+        b, cs, h = spot(i)
+        return remote(b.at[:, :, c, :, cs], b.at[:, :, c, :, cs], R.s_cs.at[i], R.s_cr.at[i], c_peer)
+
+    def kv_cols(i):
+        return pl.ds(KV + PAIR[i][1], PAIR[i][2])
+
+    def kv_over(i):
+        d = R.wide.at[:, :, c, :, kv_cols(i)]
+        return remote(d, d, R.s_xs.at[i], R.s_xr.at[i], x_peer)
+
+    def kv_core(i):
+        d = R.wide.at[:, :, c, :, kv_cols(i)]
+        return remote(d, d, R.s_cs.at[n + m + i], R.s_cr.at[n + m + i], c_peer)
+
+    def kv_core_in(i):
+        d = R.wide.at[:, :, 1 - c, :, kv_cols(i)]
+        return remote(d, d, R.s_cs.at[n + m + i], R.s_cr.at[n + m + i], c_peer)
+
+    def begin(i):
+        own_copy(i).start()
+        if i < n:
+            when(z < 3, lambda: go_right(i, 0).start())
+            when(z > 0, lambda: go_left(i, 0).start())
+        across(i, z, True).start()
+
+    def pair_turn(i):
+        own_copy(i).wait()
+        across_in(i, z).wait_recv()
+        when(z < 3, lambda: go_right(i, 0).start())
+        when(z > 0, lambda: go_left(i, 0).start())
+
+    def hop(i, s):
+        def lower():
+            from_left(i, s).wait_recv()
+            if s < 3:
+                when(z < 3, lambda: go_right(i, s).start())
+            if i < n:
+                across(i, z - s).start()
+
+        def upper():
+            from_right(i, s).wait_recv()
+            if s < 3:
+                when(z > 0, lambda: go_left(i, s).start())
+            if i < n:
+                across(i, z + s).start()
+
+        when(z >= s, lower)
+        when(z + s <= 3, upper)
+
+    def line_done(i):
+        if i < n:
+            own_copy(i).wait()
+            for zz in range(4):
+                across_in(i, zz).wait_recv()
+            to_core(i).start()
+        else:
+            when(second, lambda: to_core(i).start())
+            when(first, lambda: kv_over(i - n).start())
+
+    def have(i):
+        if i < n:
+            core_in(i).wait_recv()
+        else:
+            when(second, lambda: core_in(i).wait_recv())
+
+    def kv_turn(i):
+        kv_over(i).wait_recv()
+        kv_core(i).start()
+
+    def sent(i):
+        for s in range(3):
+            when((z >= s) & (z < 3), lambda: go_right(i, s).wait_send())
+            when((z + s <= 3) & (z > 0), lambda: go_left(i, s).wait_send())
+        for zz in range(4 if i < n else 1):
+            across(i, zz).wait_send()
+        if i < n:
+            to_core(i).wait_send()
+        else:
+            when(second, lambda: to_core(i).wait_send())
+            when(second, lambda: kv_core(i - n).wait_send())
+            when(first, lambda: kv_over(i - n).wait_send())
+
+    def tick(t):
+        for j in range(m):
+            if t == 2 * j:
+                begin(n + j)
+            if t == 2 * j + 1:
+                pair_turn(n + j)
+            for s in (1, 2, 3):
+                if t == 2 * j + 1 + s:
+                    hop(n + j, s)
+            if t == 2 * j + 5:
+                line_done(n + j)
+        if t < n:
+            begin(t)
+        for s in (1, 2, 3):
+            if 0 <= t - s < n:
+                hop(t - s, s)
+        if 0 <= t - 4 < n:
+            line_done(t - 4)
+
+    gain_own = local(gain_in, R.gz.at[z], R.s_in.at[0])
+    gain_own.start()
+    x_in = local(acts_h, R.x, R.s_in.at[1])
+    x_in.start()
+    g_in = local(cot_h, R.g, R.s_in.at[2])
+    g_in.start()
+
+    def small_z(own_ref, slots, row):
+        return [remote(own_ref, slots.at[z], R.s_gs.at[row, k], R.s_gr.at[row, k], z_peer[k]) for k in range(3)]
+
+    def small_pair(slots, row, k, dev):
+        return remote(slots.at[0], slots.at[1], R.s_gs.at[row, k], R.s_gr.at[row, k], dev)
+
+    gzc = small_z(gain_in, R.gz, 0)
+    for q in gzc:
+        q.start()
+    tick(0)
+    gain_own.wait()
+    for q in gzc:
+        q.wait_recv()
+    R.gy[0] = (R.gz[0] + R.gz[1]) + (R.gz[2] + R.gz[3])
+    q = small_pair(R.gy, 0, 3, y_peer)
+    q.start()
+    tick(1)
+    q.wait()
+    R.gc[0] = R.gy[0] + R.gy[1]
+    q = small_pair(R.gc, 0, 4, c_peer)
+    q.start()
+    q.wait()
+    R.gain[...] = R.gc[0] + R.gc[1]
+    for q in gzc:
+        q.wait_send()
+    gain = lambda k: R.gain[k : k + 1, :]
+
+    ones = jnp.where(first, 1.0, 0.0)
+    for img in range(MICRO):
+        row = jnp.broadcast_to(seg_in[img : img + 1, :].astype(F32), (SEQ, SEQ))
+        key = lax.broadcasted_iota(jnp.int32, (SEQ, SEQ), 0)
+        query = lax.broadcasted_iota(jnp.int32, (SEQ, SEQ), 1)
+        allowed = jnp.where((row.T == row) & (key <= query), 1.0, ones)
+        R.mask[img] = allowed.astype(BF)
+    R.dgain[...] = jnp.zeros_like(R.dgain)
+
+    x_in.wait()
+    norm_forward(R.x, gain(0), R.n1)
+    for t in range(2, 7):
+        tick(t)
+    have(0), have(1)
+    project(R.n1, R.wide, QKV, R.qkv, 0, 3 * D, 768)
+
+    def self_attention(a, b):
+        attend_forward(R.qkv, 0, R.qkv, D, R.qkv, 2 * D, R.ao, R.aoT, R.mask, a, b)
+
+    self_attention(0, 4)
+    tick(7)
+    self_attention(4, 8)
+    have(2)
+    tick(8)
+    self_attention(8, 12)
+    project_add(R.ao, R.wide, OP, R.x, R.mid, 384)
+    tick(9)
+
+    def enc_tiles(a, b):
+        when(first, lambda: gated_forward(R.n2, R.wide, R.gu, R.hid, a, b))
+
+    when(first, lambda: norm_forward(R.mid, gain(1), R.n2))
+    when(second, lambda: norm_forward(R.mid, gain(2), R.n3))
+    have(3), have(4)
+    enc_tiles(0, 2)
+    tick(10)
+    enc_tiles(2, 4)
+    have(5)
+    tick(11)
+    have(6)
+    enc_tiles(4, 8)
+    tick(12)
+    have(7)
+
+    def message(img):
+        rows = pl.ds(img * SEQ, SEQ)
+        return remote(R.xsend.at[rows], R.xin.at[rows], R.s_ms.at[img], R.s_mr.at[img], x_peer)
+
+    def down(base, out, cols):
+        for lo in cols:
+            cs = pl.ds(lo, 384)
+            R_w = R.tall[:, :, :, :, cs].reshape(FF, 384)
+            out[:, cs] = base[:, cs] + dot(R.hid[...], R_w)
+
+    when(first, lambda: down(R.mid, R.late, (0,)))
+    have(8)
+
+    def enc_tail():
+        down(R.mid, R.late, (384,))
+        for img in range(MICRO):
+            norm_forward(R.late, gain(2), R.xsend, img * SEQ, SEQ)
+            message(img).start()
+
+    when(first, enc_tail)
+    for j in range(m):
+        have(n + j)
+    when(second, lambda: [kv_turn(j) for j in range(m)] and None)
+    for i in range(n + m):
+        sent(i)
+
+    res_copy = local(R.late, res_o, R.s_out.at[0])
+
+    def dec_forward():
+        project(R.n3, R.wide, XA, R.xq, 0, D, 384)
+        for j in range(m):
+            kv_core_in(j).wait_recv()
+        for img in range(MICRO):
+            message(img).wait_recv()
+            project(R.xin, R.wide, KV, R.kv, 0, 2 * D, 768, img * SEQ, SEQ)
+            attend_forward(R.xq, 0, R.kv, 0, R.kv, D, R.cm, R.cmT, None, img * 6, img * 6 + 6)
+        project_add(R.cm, R.wide, XB, R.mid, R.late, 384)
+        norm_forward(R.late, gain(1), R.n2)
+        gated_forward(R.n2, R.wide, R.gu, R.hid, 0, 8)
+
+    when(second, dec_forward)
+
+    def sum_spot(name):
+        b, lo, size = SUMS[name]
+        return SUM_NAMES.index(name), b, pl.ds(lo, size), size
+
+    stage_of = {}
+
+    def core_copy(name):
+        k, b, cs, size = sum_spot(name)
+        if b == "tall":
+            s = R.stage_tall.at[:, :, :, cs]
+        else:
+            s = R.stage.at[stage_of[name], :, :, :, pl.ds(0, size)]
+        return remote(s, buf[b].at[:, :, c, :, cs], R.t_cs.at[k], R.t_cr.at[k], c_peer)
+
+    def y_copy(name):
+        k, b, cs, size = sum_spot(name)
+        return remote(buf[b].at[:, 1 - y, c, :, cs], ybuf[b].at[:, :, cs], R.t_ys.at[k], R.t_yr.at[k], y_peer)
+
+    def z_copies(name):
+        k, b, cs, size = sum_spot(name)
+        return [
+            remote(buf[b].at[lax.rem(z + j + 1, 4), y, c, :, cs], zbuf[b].at[j, :, cs], R.t_zs.at[k, j], R.t_zr.at[k, j], z_peer[j])
+            for j in range(3)
+        ]
+
+    def release(name):
+        pl.semaphore_signal(R.free.at[FREE[name]], inc=1, device_id=c_peer, device_id_type=MESH)
+
+    def claim(name):
+        pl.semaphore_wait(R.free.at[FREE[name]], 1)
+
+    order = []
+
+    def grad_wide(name, nT, g_ref, gcol, tile):
+        k, b, cs, size = sum_spot(name)
+        lo = SUMS[name][1]
+        slot = len(order) % 2
+        if len(order) >= 2:
+            core_copy(order[-2]).wait_send()
+        stage_of[name] = slot
+        order.append(name)
+        lhs = half_rows(nT, 1 - c)
+
+        @pl.loop(0, size // tile)
+        def _(j):
+            w = dot(lhs, g_ref[:, pl.ds(mul(gcol + j * tile, 128), tile)]).astype(BF)
+            R.stage[slot, :, :, :, pl.ds(mul(j * tile, 128), tile)] = w.reshape(4, 2, 48, tile)
+
+        core_copy(name).start()
+        mine = half_rows(nT, c)
+
+        @pl.loop(0, size // tile)
+        def _(j):
+            w = dot(mine, g_ref[:, pl.ds(mul(gcol + j * tile, 128), tile)]).astype(BF)
+            R.wide[:, :, c, :, pl.ds(mul(lo + j * tile, 128), tile)] = w.reshape(4, 2, 48, tile)
+
+    def drain():
+        for name in order[-2:]:
+            core_copy(name).wait_send()
+        order.clear()
+
+    def grad_tall():
+        def rows_of(j, cc):
+            units = pl.ds(mul((2 * j + cc) * 128, 128), 128)
+            return dot(R.hid[:, units].T, R.gb[...]).astype(BF)
+
+        @pl.loop(0, 8)
+        def _(j):
+            R.stage_tall[j // 2, j % 2] = rows_of(j, 1 - c)
+
+        core_copy("out0").start()
+        core_copy("out1").start()
+
+        @pl.loop(0, 8)
+        def _(j):
+            R.tall[j // 2, j % 2, c] = rows_of(j, c)
+
+    def core_stage(name, pass_on=True):
+        k, b, cs, size = sum_spot(name)
+        w = buf[b]
+        landed = w.at[:, :, 1 - c, :, cs]
+        remote(landed, landed, R.t_cs.at[k], R.t_cr.at[k], c_peer).wait_recv()
+
+        @pl.loop(0, 8)
+        def _(j):
+            own = w[j // 2, j % 2, c, :, cs].astype(F32)
+            w[j // 2, j % 2, c, :, cs] = (own + w[j // 2, j % 2, 1 - c, :, cs].astype(F32)).astype(BF)
+
+        if pass_on:
+            y_copy(name).start()
+
+    def y_stage(name):
+        k, b, cs, size = sum_spot(name)
+        y_copy(name).wait_recv()
+        w, r = buf[b], ybuf[b]
+
+        @pl.loop(0, 4)
+        def _(j):
+            w[j, y, c, :, cs] = (w[j, y, c, :, cs].astype(F32) + r[j, :, cs].astype(F32)).astype(BF)
+
+        for q in z_copies(name):
+            q.start()
+
+    finished = []
+
+    def out_copy(name):
+        k, b, cs, size = sum_spot(name)
+        arg, lo = OUT_OF[name]
+        kind = [f for f in finished if SUMS[f][0] == b]
+        slot = kind.index(name) % 2
+        f = R.fin_tall.at[slot] if b == "tall" else R.fin.at[slot, :, pl.ds(0, size)]
+        return local(f, dst[arg].at[:, pl.ds(lo, size)], R.t_out.at[k])
+
+    def z_stage(name):
+        k, b, cs, size = sum_spot(name)
+        for q in z_copies(name):
+            q.wait_recv()
+        kind = [f for f in finished if SUMS[f][0] == b]
+        slot = len(kind) % 2
+        if len(kind) >= 2:
+            out_copy(kind[-2]).wait()
+        finished.append(name)
+        r = zbuf[b]
+        total = (buf[b][z, y, c, :, cs].astype(F32) + r[0, :, cs].astype(F32)) + (
+            r[1, :, cs].astype(F32) + r[2, :, cs].astype(F32)
+        )
+        if b == "tall":
+            R.fin_tall[slot] = total
+        else:
+            R.fin[slot, :, pl.ds(0, size)] = total
+        out_copy(name).start()
+
+    def over_copy(j):
+        k, b, cs, size = sum_spot(("k0", "k1")[j])
+        return remote(
+            R.wide.at[:, :, c, :, cs], R.wide.at[:, :, c, :, pl.ds(XA + j * D, D)], R.t_xs.at[j], R.t_xr.at[j], x_peer
+        )
+
+    def round_g():
+        R.gb[...] = R.g[...].astype(BF)
+
+    g_in.wait()
+
+    def enc_entry():
+        for img in range(MICRO):
+            message(img).wait_send()
+        res_copy.start()
+        for img in range(MICRO):
+            message(img).wait_recv()
+        R.acc[...] = R.xin[...].astype(F32)
+        norm_backward(R.late, gain(2), R.acc, R.g, R.dgain, 2)
+
+    when(first, enc_entry)
+    round_g()
+    def dec_late():
+        down(R.late, R.acc, (0, 384))
+
+    dec_res_copy = local(R.acc, res_o, R.s_out.at[0])
+
+    def dec_result():
+        dec_late()
+        dec_res_copy.start()
+
+    when(second, dec_result)
+    gated_backward(R.gb, R.tall, R.gu, 0, 8)
+    release("out")
+    claim("out")
+    grad_tall()
+    when(second, lambda: dec_res_copy.wait())
+    back_project(R.gu, 0, R.wide, WIN, 2 * FF, 512, R.acc)
+    release("in")
+    core_stage("out0")
+    core_stage("out1")
+    when(first, lambda: res_copy.wait())
+    when(first, lambda: norm_backward(R.mid, gain(1), R.acc, R.g, R.dgain, 1))
+    when(second, lambda: norm_backward(R.late, gain(1), R.acc, R.g, R.dgain, 1))
+    transpose_to(R.n2, R.nT)
+    claim("in")
+    grad_wide("in0", R.nT, R.gu, 0, 512)
+    grad_wide("in1", R.nT, R.gu, 1024, 512)
+    core_stage("in0")
+    grad_wide("in2", R.nT, R.gu, FF, 512)
+    core_stage("in1")
+    grad_wide("in3", R.nT, R.gu, FF + 1024, 512)
+    core_stage("in2")
+    round_g()
+
+    def project_back(g_ref, wcol, out_ref):
+        out_ref[...] = dot(g_ref[...], wide_cols(R.wide, wcol, D), NT).astype(BF)
+
+    def dec_cross():
+        project_back(R.gb, XB, R.xsend)
+        for img in range(MICRO):
+            attend_backward(
+                R.xq, 0, R.kv, 0, R.kv, D, R.xsend, None, R.xq, 0, R.kv, 0, R.kv, D, img * 6, img * 6 + 6
+            )
+            back_project(R.kv, 0, R.wide, KV, 2 * D, 768, R.acc, img * SEQ, SEQ)
+            rows = pl.ds(img * SEQ, SEQ)
+            R.xsend[rows, :] = R.acc[rows, :].astype(BF)
+            message(img).start()
+
+    when(second, dec_cross)
+    core_stage("in3")
+    y_stage("out0")
+    y_stage("out1")
+
+    def dec_cross_grads():
+        release("k")
+        transpose_to(R.xin, R.nT)
+        claim("k")
+        grad_wide("k0", R.nT, R.kv, 0, 384)
+        grad_wide("k1", R.nT, R.kv, D, 384)
+        back_project(R.xq, 0, R.wide, XA, D, 768, R.acc)
+        release("x")
+        core_stage("k0", False)
+        over_copy(0).start()
+        core_stage("k1", False)
+        over_copy(1).start()
+        transpose_to(R.n3, R.nT)
+        claim("x")
+        grad_wide("x0", R.nT, R.xq, 0, 384)
+        grad_wide("x1", R.cmT, R.gb, 0, 384)
+        norm_backward(R.mid, gain(2), R.acc, R.g, R.dgain, 2)
+        core_stage("x0")
+        core_stage("x1")
+        for img in range(MICRO):
+            message(img).wait_send()
+        drain()
+        round_g()
+
+    drain()
+    when(second, dec_cross_grads)
+    y_stage("in0")
+
+    project_back(R.gb, OP, R.ao)
+    release("o")
+    attend_backward(R.qkv, 0, R.qkv, D, R.qkv, 2 * D, R.ao, R.mask, R.qkv, 0, R.qkv, D, R.qkv, 2 * D, 0, 6)
+    y_stage("in1")
+    attend_backward(R.qkv, 0, R.qkv, D, R.qkv, 2 * D, R.ao, R.mask, R.qkv, 0, R.qkv, D, R.qkv, 2 * D, 6, 12)
+    back_project(R.qkv, 0, R.wide, QKV, 3 * D, 768, R.acc)
+    release("q")
+    y_stage("in2")
+    claim("o")
+    grad_wide("o", R.aoT, R.gb, 0, 384)
+    transpose_to(R.n1, R.nT)
+    claim("q")
+    grad_wide("q0", R.nT, R.qkv, 0, 384)
+    core_stage("o")
+    grad_wide("q1", R.nT, R.qkv, 1152, 384)
+    core_stage("q0")
+    core_stage("q1")
+    norm_backward(R.x, gain(0), R.acc, R.g, R.dgain, 0)
+    grad_copy = local(R.g, grad_o, R.s_out.at[1])
+    grad_copy.start()
+
+    def enc_x():
+        for j in range(2):
+            over_copy(j).wait_recv()
+            y_copy(("x0", "x1")[j]).start()
+
+    when(first, enc_x)
+
+    R.hc[0] = R.dgain[...]
+    q = small_pair(R.hc, 1, 4, c_peer)
+    q.start()
+    q.wait()
+    R.hy[0] = R.hc[0] + R.hc[1]
+    q = small_pair(R.hy, 1, 3, y_peer)
+    q.start()
+    q.wait()
+    R.gain[...] = R.hy[0] + R.hy[1]
+    hzc = small_z(R.gain, R.hz, 1)
+    for q in hzc:
+        q.start()
+
+    y_stage("in3")
+    z_stage("out0")
+    z_stage("out1")
+    y_stage("x0")
+    z_stage("in0")
+    y_stage("x1")
+    z_stage("in1")
+    y_stage("o")
+    z_stage("in2")
+    z_stage("in3")
+    y_stage("q0")
+    z_stage("x0")
+    z_stage("x1")
+    y_stage("q1")
+    z_stage("o")
+    z_stage("q0")
+    z_stage("q1")
+    for q in hzc:
+        q.wait()
+    R.hz[z] = R.gain[...]
+    R.dgain[...] = (R.hz[0] + R.hz[1]) + (R.hz[2] + R.hz[3])
+    gain_copy = local(R.dgain, gain_o, R.s_out.at[2])
+    gain_copy.start()
+    for name in ("out0", "out1"):
+        core_copy(name).wait_send()
+    drain()
+    for name in finished:
+        y_copy(name).wait_send()
+        for q in z_copies(name):
+            q.wait_send()
+    when(second, lambda: [over_copy(j).wait_send() for j in range(2)] and None)
+    for b in ("tall", "wide"):
+        for name in [f for f in finished if SUMS[f][0] == b][-2:]:
+            out_copy(name).wait()
+    grad_copy.wait()
+    gain_copy.wait()
 
 
 def from_behind(block, axis, distance):
@@ -25,7 +863,7 @@
     )
 
 
-def project(left_side, right_side):
+def product(left_side, right_side):
     return jnp.dot(left_side, right_side, preferred_element_type=jnp.float32)
 
 
@@ -55,7 +893,7 @@
     return jnp.where(allowed[None], raw_logits, -1e30)
 
 
-def attend_forward(queries, keys_in, values, allowed):
+def attend_plain(queries, keys_in, values, allowed):
     logits = logits_of(queries, keys_in, allowed)
     row_peak = jnp.max(logits, axis=-1, keepdims=True)
     weights = jnp.exp(logits - row_peak)
@@ -70,7 +908,7 @@
     )
 
 
-def attend_backward(queries, keys_in, values, allowed, log_total, grad_mixed):
+def attend_plain_back(queries, keys_in, values, allowed, log_total, grad_mixed):
     softmax_out = jnp.exp(logits_of(queries, keys_in, allowed) - log_total)
     grad_heads = heads_of(grad_mixed)
     grad_softmax = jnp.einsum(
@@ -101,12 +939,12 @@
 
 def self_forward(inputs, gain_row, w_attn, allowed):
     normed = rms_norm(inputs, gain_row).astype(jnp.bfloat16)
-    packed = project(normed, w_attn[:, : 3 * D]).astype(jnp.bfloat16)
-    mixed_heads, log_total = attend_forward(
+    packed = product(normed, w_attn[:, : 3 * D]).astype(jnp.bfloat16)
+    mixed_heads, log_total = attend_plain(
         packed[:, :D], packed[:, D : 2 * D], packed[:, 2 * D :], allowed
     )
     return (
-        inputs + project(mixed_heads, w_attn[:, 3 * D :]),
+        inputs + product(mixed_heads, w_attn[:, 3 * D :]),
         (normed, packed, mixed_heads, log_total),
     )
 
@@ -116,7 +954,7 @@
     grad_low = grad_result.astype(jnp.bfloat16)
     grad_proj = weight_grad(mixed_heads, grad_low)
     grad_mixed = input_back(grad_low, w_attn[:, 3 * D :]).astype(jnp.bfloat16)
-    grad_queries, grad_keys, grad_values = attend_backward(
+    grad_queries, grad_keys, grad_values = attend_plain_back(
         packed[:, :D], packed[:, D : 2 * D], packed[:, 2 * D :], allowed, log_total, grad_mixed
     )
     grad_packed = jnp.concatenate([grad_queries, grad_keys, grad_values], axis=1).astype(
@@ -135,9 +973,9 @@
 
 def ffn_forward(inputs, gain_row, w_in, w_out):
     normed = rms_norm(inputs, gain_row).astype(jnp.bfloat16)
-    gated = project(normed, w_in)
+    gated = product(normed, w_in)
     hidden = gated_unit(gated).astype(jnp.bfloat16)
-    return (inputs + project(hidden, w_out), (normed, gated, hidden))
+    return (inputs + product(hidden, w_out), (normed, gated, hidden))
 
 
 def ffn_backward(inputs, gain_row, w_in, w_out, kept_values, grad_result):
@@ -156,7 +994,7 @@
     middle, first_kept = self_forward(inputs, gain_rows[0], w_attn, None)
     result, second_kept = ffn_forward(middle, gain_rows[1], w_in, w_out)
     normed = rms_norm(result, gain_rows[2]).astype(jnp.bfloat16)
-    cross_kv = project(normed, w_extra).astype(jnp.bfloat16)
+    cross_kv = product(normed, w_extra).astype(jnp.bfloat16)
     return (result, cross_kv, (middle, first_kept, second_kept, normed))
 
 
@@ -188,9 +1026,9 @@
     w_attn, w_extra, w_in, w_out, gain_rows = weights
     middle, first_kept = self_forward(inputs, gain_rows[0], w_attn, allowed)
     query_in = rms_norm(middle, gain_rows[2]).astype(jnp.bfloat16)
-    queries = project(query_in, w_extra[:, :D]).astype(jnp.bfloat16)
-    mixed_heads, log_total = attend_forward(queries, cross_kv[:, :D], cross_kv[:, D:], None)
-    after_cross = middle + project(mixed_heads, w_extra[:, D:])
+    queries = product(query_in, w_extra[:, :D]).astype(jnp.bfloat16)
+    mixed_heads, log_total = attend_plain(queries, cross_kv[:, :D], cross_kv[:, D:], None)
+    after_cross = middle + product(mixed_heads, w_extra[:, D:])
     result, second_kept = ffn_forward(after_cross, gain_rows[1], w_in, w_out)
     grad_after, gain_late, grad_win, grad_wout = ffn_backward(
         after_cross, gain_rows[1], w_in, w_out, second_kept, grad_result
@@ -198,7 +1036,7 @@
     grad_low = grad_after.astype(jnp.bfloat16)
     grad_cross_out = weight_grad(mixed_heads, grad_low)
     grad_mixed = input_back(grad_low, w_extra[:, D:]).astype(jnp.bfloat16)
-    grad_queries, grad_keys, grad_values = attend_backward(
+    grad_queries, grad_keys, grad_values = attend_plain_back(
         queries, cross_kv[:, :D], cross_kv[:, D:], None, log_total, grad_mixed
     )
     grad_queries = grad_queries.astype(jnp.bfloat16)
@@ -220,7 +1058,7 @@
     return (result, grad_inputs, grad_kv, gradients)
 
 
-def local(acts, w_attn, w_extra, w_in, w_out, gains, segments, cotangent):
+def general(acts, w_attn, w_extra, w_in, w_out, gains, segments, cotangent):
     gathered = (
         lax.all_gather(w_attn[0], "dp", axis=0, tiled=True),
         lax.all_gather(w_extra[0], "dp", axis=0, tiled=True),
@@ -299,6 +1137,35 @@
     )
 
 
+def step(acts, w_attn, w_extra, w_in, w_out, gains, segments, cotangent):
+    me = lax.axis_index("dp")
+    share = gains.shape[2]
+    own_gain = lax.dynamic_update_slice(jnp.zeros((8, D), F32), gains[0].astype(F32), (0, me * share))
+    anywhere = pl.BlockSpec(memory_space=pl.ANY)
+    shape = lambda *s: jax.ShapeDtypeStruct(s, F32)
+    scratch = scratch_list()
+    results, input_grad, attn, extra, win, wout, gain = pl.pallas_call(
+        whole_kernel,
+        out_shape=(
+            shape(ROWS, D), shape(ROWS, D), shape(48, 4 * D), shape(48, 2 * D), shape(48, 2 * FF), shape(128, D), shape(8, D),
+        ),
+        in_specs=[anywhere] * 7 + [pl.BlockSpec(memory_space=pltpu.VMEM)],
+        out_specs=[anywhere] * 7,
+        scratch_shapes=list(scratch.values()),
+        compiler_params=pltpu.CompilerParams(
+            collective_id=0, has_side_effects=True, vmem_limit_bytes=63 * 2**20
+        ),
+    )(
+        acts.reshape(ROWS, D), cotangent.reshape(ROWS, D), w_attn[0], w_extra[0], w_in[0], w_out[0], own_gain,
+        segments.reshape(MICRO, SEQ),
+    )
+    grad_gains = lax.dynamic_slice(gain, (0, me * share), (3, share))
+    like = (1, MICRO, 1, SEQ, D)
+    return (
+        results.reshape(like), input_grad.reshape(like), attn[None], extra[None], win[None], wout[None], grad_gains[None],
+    )
+
+
 def solution(mesh):
     in_specs = (
         P("section", None, "dp", None, None),
@@ -319,4 +1186,5 @@
         P("section", "dp", None),
         P("section", None, "dp"),
     )
-    return jax.shard_map(local, mesh=mesh, in_specs=in_specs, out_specs=out_specs, check_vma=False)
+    fits = mesh.shape["dp"] == 16
+    return jax.shard_map(step if fits else general, mesh=mesh, in_specs=in_specs, out_specs=out_specs, check_vma=False)

time: 1150 us -> 354 us (0.31)
  waiting for transfers between devices: 707 us -> 0 us
  Pallas kernels: 0 us -> 342 us
  matrix products: 153 us -> 0 us
  starting transfers between devices: 91.8 us -> 0 us
  other arithmetic: 82.3 us -> 0.68 us
  local copies, waits for them, and re-layouts: 51.1 us -> 10.2 us
  blocking collectives: 24.5 us -> 0 us
  loops' own time: 18 us -> 0 us
  between operations: 14.4 us -> 0.67 us
    reduce_scatter x4 -> x0, waiting for transfers between devices: 422 us -> none  [the longest x1 139 us: local(): lax.psum_scatter(totals[2], 'dp', scatter_dimension=0, tiled=True)]
    pallas_call x0 -> x1, Pallas kernels: none -> 342 us  [step(): pl.pallas_call(whole_kernel, out_shape=(shape(ROWS, D), shape(ROWS, D), s...]
    all_gather x4 -> x0, waiting for transfers between devices: 183 us -> none  [the longest x1 62.6 us: local(): lax.all_gather(w_in[0], 'dp', axis=0, tiled=True)]
    dot_general x51 -> x0, matrix products: 141 us -> none  [the longest x9 39 us: weight_grad(): jnp.einsum('sd,se->de', left_side, right_side, preferred_element_type=jnp...]
    ppermute x4 -> x0, waiting for transfers between devices: 98.8 us -> none  [from_behind(): return lax.ppermute(block, axis, route)]
    ppermute x4 -> x0, starting transfers between devices: 91.5 us -> none  [from_behind(): return lax.ppermute(block, axis, route)]
    add x11 -> x0, other arithmetic: 55.3 us -> none  [the longest x5 53.2 us: local(): totals = tuple((jnp.add(*couple) for couple in zip(totals, fresh_grads)))]
    all_gather x1 -> x0, blocking collectives: 24.5 us -> none  [local(): lax.all_gather(gains[0], 'dp', axis=1, tiled=True)]
  transfers between devices with their start and end apart: 13 -> 0, of which waited for: 13 -> 0; matrix products, arithmetic and copies ran while one was open for 5% -> 0% of each run, Pallas kernels for 0% -> 0%
where the time goes in v1:
time: 354 us
  Pallas kernels  342 us (97%)
  local copies, waits for them, and re-layouts  10.2 us (3%)
    pallas_call x1, Pallas kernels, step(): pl.pallas_call(whole_kernel, out_shape=(shape(ROWS, D), shape(ROWS, D), s...  342 us
    unnamed x19, local copies, waits for them, and re-layouts  8.65 us

profile of v1, /device:TPU:0, one launch (start us, length us, event | category | flops | bytes accessed | tf_op | source)
XLA Modules:
  0.0 353.8 jit_solution(14181123884078728810)
XLA Ops:
  0.6 0.7 bitcast_convert_fusion
  1.3 0.2 dynamic_update_slice.3.refs_6_
  1.6 0.0 copy-start.5
  1.6 1.3 copy.19
  2.9 0.0 copy-done.5
  2.9 342.2 %shard_map.135 = (f32[512,768]{1,0:T(8,128)}, f32[512,768]{1,0:T(8,128)}, f32[48,3072]{1,0:T(8,128)}, f32[48,1536]{1,0:T(8,128)}, f32[48,4096]{1,0:T(8,128)}, /*index=5*/f32[128,768]{1,0:T(8,128)}, f32[8,768]{1,0:T(8,128)}) custom-call(f32[512,768]{1,0:T(8,128)} %bitcast.24, f32[512,768]{1,0:T(8,128)} %bitcast.25, bf16[48,3072]{1,0:T(8,128)(2,1)} %bitcast.31, ...), custom_call_target="tpu_custom_call" | custom-call | tf_op jit(solution)/shard_map/pallas_call | solution.py:1147
  345.1 0.8 constant_dynamic-slice_fusion
  345.8 0.6 broadcast_in_dim.23
  346.4 0.0 copy-start
  346.4 2.8 copy.27
  349.2 0.0 copy-done
  349.2 0.0 copy-start.2
  349.2 0.0 copy-start.4
  349.2 1.1 copy.28
  350.3 0.3 copy-done.2
  350.6 0.0 copy-start.1
  350.6 0.0 copy-start.3
  350.6 0.8 copy.29
  351.4 0.0 copy-done.4
  351.4 0.7 copy.30
  352.2 0.0 copy-done.1
  352.2 0.9 copy.31
  353.0 0.0 copy-done.3
  353.0 0.7 copy.32
  (1 shorter events, 0.0 us)
Async XLA Ops:
  1.6 1.3 copy-start.5
  346.4 2.8 copy-start
  349.2 1.4 copy-start.2
  349.2 2.3 copy-start.4
  350.6 1.5 copy-start.1
  350.6 2.4 copy-start.3
